TPU v7x, 256 devices: a whole 4x4x8 slice. The times are simulated.
256 devices in a mesh: rep: 4 (over y_hi, core), fsdp: 64 (over z, y_lo, x).
Axes of the slice: x: 4, y: 4 (y_hi: 2, y_lo: 2; y = y_hi * 2 + y_lo), z: 8, core: 2. Of those that a mesh axis runs over, the one named last changes fastest.
Arguments:
- inputs: bfloat16 [4, 49152, 2304], P('rep', 'fsdp'), may hold values from -6 to 6
- cotangent: bfloat16 [4, 49152, 2304], P('rep', 'fsdp'), may hold values from -6 to 6
- replica_params: float32 [4, 1024, 2, 2304], P('rep', 'fsdp'), as said below
- anchor: float32 [1024, 2, 2304], P('fsdp'), as said below
- momentum: float32 [3, 1024, 2, 768], P(None, 'fsdp', None, 'rep'), may hold values from -2 to 2
- fragment: int32 [1], replicated, may hold values from 0 to 2
Outputs:
- replica_new: float32 [4, 1024, 2, 2304], P('rep', 'fsdp')
- anchor_new: float32 [1024, 2, 2304], P('fsdp')
- momentum_new: float32 [3, 1024, 2, 768], P(None, 'fsdp', None, 'rep')
Inputs may be any that keep to these rules, and one draw needn't show every extreme that they name: `replica_params`: each replica's parameters are the anchor plus an independent drift with entries of deviation 0.3. `anchor`: entries of deviation 1.
All inputs are finite; a program needn't handle non-finite values.
Results may differ from a plain program's by a relative error of at most 0.0026.
Values may be sent and summed in bfloat16 or wider, within the bound.
A program may use at most 128 MiB of HBM per device.

v0:
```python
import math

import jax
import jax.numpy as jnp
from jax import lax
from jax.sharding import PartitionSpec as P

DW = 2304
HV = 1024
NFRAG = 3


inner_rate = 0.5
outer_rate = 0.7
outer_momentum = 0.9
norm_epsilon = 1e-06


def grad_terms(values, back_values, normed, cotangent_rows, scale):

    def term(start, count):
        grad_value = jnp.einsum(
            "tk,td->kd", back_values, normed, preferred_element_type=jnp.float32
        )
        grad_output = jnp.einsum(
            "tk,td->kd", values, cotangent_rows, preferred_element_type=jnp.float32
        )
        return jnp.stack([grad_value, grad_output], axis=1) * scale

    return term


def outer_update(pseudo, anchor_frag, moment_piece):
    replicas = lax.axis_size("rep")
    quarter = moment_piece.shape[2]
    delta = lax.psum_scatter(pseudo, "rep", scatter_dimension=2, tiled=True) / replicas
    new_piece_moment = outer_momentum * moment_piece + delta
    own = lax.axis_index("rep") * quarter
    anchor_piece = lax.dynamic_slice_in_dim(anchor_frag, own, quarter, 2)
    new_piece = anchor_piece - outer_rate * (delta + outer_momentum * new_piece_moment)
    new_frag = lax.all_gather(new_piece, "rep", axis=2, tiled=True)
    return (new_frag, new_piece_moment)


def per_device(inputs, cotangent, replica_params, anchor, momentum, fragment):
    rows_in = inputs[0]
    cotangent_rows = cotangent[0]
    params = replica_params[0]
    rows_dev = params.shape[0]
    width = params.shape[2]
    frag_width = width // NFRAG
    wide = rows_in.astype(jnp.float32)
    normed = (
        wide * lax.rsqrt(jnp.mean(wide * wide, axis=-1, keepdims=True) + norm_epsilon)
    ).astype(jnp.bfloat16)
    weights16 = params.astype(jnp.bfloat16)
    piece = lax.all_gather(weights16, "fsdp", axis=0, tiled=True)
    vals = jnp.einsum(
        "td,kd->tk", normed, piece[:, 0, :], preferred_element_type=jnp.float32
    ) / math.sqrt(DW)
    backs = jnp.einsum(
        "td,kd->tk", cotangent_rows, piece[:, 1, :], preferred_element_type=jnp.float32
    ) / math.sqrt(HV)
    both = jnp.stack([vals, backs]).astype(jnp.bfloat16)
    values = both[0]
    back_values = both[1]
    scale = 1.0 / math.sqrt(rows_in.shape[0] * lax.axis_size("fsdp"))
    index = fragment[0]
    offset = index * frag_width
    anchor_frag = lax.dynamic_slice_in_dim(anchor, offset, frag_width, 2)
    moment_piece = lax.dynamic_index_in_dim(momentum, index, 0, keepdims=False)
    term = grad_terms(values, back_values, normed, cotangent_rows, scale)
    grads = lax.psum_scatter(
        term(jnp.int32(0), rows_dev * lax.axis_size("fsdp")),
        "fsdp",
        scatter_dimension=0,
        tiled=True,
    )
    inner = params - inner_rate * grads
    inner_frag = lax.dynamic_slice_in_dim(inner, offset, frag_width, 2)
    new_frag, new_piece_moment = outer_update(anchor_frag - inner_frag, anchor_frag, moment_piece)
    zero = jnp.zeros((), jnp.int32)
    momentum_new = lax.dynamic_update_index_in_dim(momentum, new_piece_moment, index, 0)
    anchor_new = lax.dynamic_update_slice(anchor, new_frag, (zero, zero, offset))
    replica_new = lax.dynamic_update_slice(inner, new_frag, (zero, zero, offset))
    return (replica_new[None], anchor_new, momentum_new)


def solution(mesh):
    return jax.shard_map(
        per_device,
        mesh=mesh,
        in_specs=(
            P("rep", "fsdp", None),
            P("rep", "fsdp", None),
            P("rep", "fsdp", None, None),
            P("fsdp", None, None),
            P(None, "fsdp", None, "rep"),
            P(),
        ),
        out_specs=(
            P("rep", "fsdp", None, None),
            P("fsdp", None, None),
            P(None, "fsdp", None, "rep"),
        ),
        check_vma=False,
    )
```

profile of v0, /device:TPU:1, one launch (start us, length us, event | category | flops | bytes accessed | tf_op | source)
XLA Modules:
  0.0 786.6 jit_solution(2402203645892981563)
XLA Ops:
  7.2 0.0 copy-start
  7.2 0.0 all-gather.2.cloned.1.call-start
  7.2 1.8 copy.51
  9.1 1.5 copy.52
  10.6 1.6 copy.44
  12.3 0.0 all-gather.2.cloned.1.call-update
  12.3 0.0 reduce-scatter.5.cloned.1.call-start
  12.3 2.8 fusion
  15.1 278.3 %all-gather.2.cloned.1.call-done = bf16[1024,2,2304]{2,0,1:T(8,128)(2,1)} async-done(((bf16[16,2,2304]{2,0,1:T(8,128)(2,1)}), bf16[1024,2,2304]{2,0,1:T(8,128)(2,1)}) %all-gather.2.cloned.1.call-update) | async-done | bytes 9437200 | tf_op jit(solution)/shard_map/all_gather | solution.py:57
  293.4 7.3 multiply_convert_fusion
  300.7 0.0 copy-done
  300.7 4.0 convolution_bitcast_fusion
  304.8 0.0 copy-start.1
  304.8 6.3 multiply_convert_fusion.1
  311.1 0.0 copy-done.1
  311.1 4.4 convolution_bitcast_fusion.1
  315.5 6.8 maximum_multiply_fusion
  322.3 0.0 reduce-scatter.5.cloned.1.call-update
  322.3 0.0 reduce-scatter.7.cloned.1.call-start
  323.1 1.5 constant_dynamic-slice_fusion.1
  324.6 346.2 %reduce-scatter.5.cloned.1.call-done = f32[16,2,2304]{2,0,1:T(8,128)} async-done(((f32[1024,2,2304]{2,0,1:T(8,128)}), f32[16,2,2304]{2,0,1:T(8,128)}) %reduce-scatter.5.cloned.1.call-update) | async-done | bytes 294928 | tf_op jit(solution)/shard_map/reduce_scatter | solution.py:73
  670.8 1.1 bitcast_subtract_fusion
  671.9 0.0 copy-start.2
  671.9 0.7 copy-done.2
  672.6 1.5 copy_subtract_fusion
  674.2 1.9 copy.25
  676.1 2.3 reshape.38
  678.4 0.0 reduce-scatter.7.cloned.1.call-update
  678.5 1.5 constant_dynamic-slice_fusion.2
  680.0 1.4 constant_dynamic-slice_fusion
  681.4 71.3 %reduce-scatter.7.cloned.1.call-done = f32[192,32]{1,0:T(8,128)} async-done(((f32[768,32]{1,0:T(8,128)}), f32[192,32]{1,0:T(8,128)}) %reduce-scatter.7.cloned.1.call-update) | async-done | bytes 24592
  752.6 1.7 reshape.39
  754.4 1.6 copy.26
  756.0 1.4 fusion.13
  757.4 1.6 copy.20
  759.0 10.9 %all_gather.7 = f32[16,2,768]{0,1,2:T(2,128)} all-gather(f32[16,2,192]{0,1,2:T(2,128)} %copy.20), channel_id=1, replica_groups=mesh['rep'=4,'fsdp'=64] {'rep'}, dimensions={2}, use_global_device_ids=true | all-gather | bytes 122880 | tf_op jit(solution)/shard_map/all_gather | solution.py:41
  769.9 1.9 copy.21
  771.8 1.9 copy.22
  773.6 1.5 bitcast_dynamic-update-slice_fusion
  775.2 1.9 copy.24
  777.1 1.5 constant_dynamic-update-slice_fusion
  778.6 1.4 copy_dynamic-update-slice_fusion
  (1 shorter events, 0.0 us)
Async XLA Ops:
  7.2 293.6 %copy-start = (bf16[1,768,2304]{2,1,0:T(8,128)(2,1)S(1)}, bf16[1,768,2304]{2,1,0:T(8,128)(2,1)}, u32[]{:S(2)}) copy-start(bf16[1,768,2304]{2,1,0:T(8,128)(2,1)} %param.7) | copy-start | bytes 10616836
  7.2 286.3 %all-gather.2.cloned.1.call-start = ((), (), s32[]{:S(2)}) async-start(), calls=%async_computation.2 | async-start | bytes 9584640 | tf_op jit(solution)/shard_map/all_gather | solution.py:57
  12.3 658.5 %reduce-scatter.5.cloned.1.call-start = ((), (), s32[]{:S(2)}) async-start(), calls=%async_computation.3 | async-start | bytes 19169280 | tf_op jit(solution)/shard_map/reduce_scatter | solution.py:73
  304.8 6.3 copy-start.1
  322.3 430.3 %reduce-scatter.7.cloned.1.call-start = ((), (), s32[]{:S(2)}) async-start(), calls=%async_computation.4 | async-start | bytes 491520
  671.9 0.7 copy-start.2
Sparse Core Ops, SparseCore 0:
  12.4 280.9 all-gather.1
  322.5 348.3 reduce-scatter.4
  678.6 74.0 reduce-scatter.6
where the time goes:
time: 788 us; the launch traced here: 787 us
  waiting for transfers between devices  696 us (88%)
  local copies, waits for them, and re-layouts  29.5 us (4%)
  matrix products  22 us (3%)
  between operations  14.5 us (2%)
  other arithmetic  13.6 us (2%)
  blocking collectives  10.9 us (1%)
    reduce_scatter x1, waiting for transfers between devices, per_device(): lax.psum_scatter(term(jnp.int32(0), rows_dev * lax.axis_size('fsdp')), 'f...  346 us
    all_gather x1, waiting for transfers between devices, per_device(): piece = lax.all_gather(weights16, 'fsdp', axis=0, tiled=True)  278 us
    unnamed x4, waiting for transfers between devices  71.3 us
  transfers between devices with their start and end apart: 3, of which 3 were waited for; matrix products, arithmetic and copies ran while one was open for 1% of the time, Pallas kernels for 0%

commit v1 on v0

v1 whole, which is shorter than its diff:
```python
import functools
import math

import jax
import jax.numpy as jnp
from jax import lax
from jax.experimental import pallas as pl
from jax.experimental.pallas import tpu as pltpu
from jax.sharding import PartitionSpec as P

DW = 2304
HV = 1024
NFRAG = 3
FRAGW = DW // NFRAG
TOKENS = 49152
ROWS = 16
TOK = 768
PAIR = 2 * TOK
CZ = 1024
CY = DW - CZ
Z, Y, X = 8, 2, 4

inner_rate = 0.5
outer_rate = 0.7
outer_momentum = 0.9
norm_epsilon = 1e-06

MESH = pl.DeviceIdType.MESH
F32 = jnp.float32
BF16 = jnp.bfloat16
ZS = pl.ds(0, CZ)
YS = pl.ds(CZ, CY)
ORDER = (4, 3, 5, 2, 6, 1, 7, 0)


def kernel(inp, cot, params, anchor, moment, frag, inner_o, delta_o, moms_o,
           toks, own, wts, wown, vals, grad, rz, sz, ry, sy, r2, fs, fr, fx, xs, osend, orecv, moms,
           load_s, tok_s, tok_r, fwd_s, fwd_r, wx_s, wx_r, ay_s, ay_r, az_s, az_r, bz_s, bz_r, by_s, by_r,
           cz_s, cz_r, cy_s, cy_r, dz_s, dz_r, dy_s, dy_r, ex_s, ex_r, om_s, om_r, of_s, of_r):
    rep = lax.axis_index("rep")
    f = lax.axis_index("fsdp")
    hi, c = rep // 2, rep % 2
    z, y, x = f // 8, (f // 4) % 2, f % 4
    kx, xh = x % 2, x // 2
    nat = 1 - (c + kx) % 2
    is_nat = nat == 1
    yo = 1 - y

    def fid(zz, yy, xx):
        return (zz % Z) * 8 + yy * 4 + xx % X

    def zat(offset):
        return (z + offset) % Z

    sib = (2 * hi + 1 - c, f)
    zdev = ((rep, fid(z + 1, y, x)), (rep, fid(z + 7, y, x)))
    ydev = (rep, fid(z, yo, x))
    peers = (sib, (2 * (1 - hi) + c, f), (2 * (1 - hi) + 1 - c, f))

    pending = []

    def send(src, dst, ssem, rsem, dev):
        cp = pltpu.make_async_remote_copy(src_ref=src, dst_ref=dst, send_sem=ssem, recv_sem=rsem,
                                          device_id=dev, device_id_type=MESH)
        cp.start()
        pending.append(cp)
        return cp

    def recv(region, ssem, rsem):
        pltpu.make_async_remote_copy(src_ref=region, dst_ref=region, send_sem=ssem, recv_sem=rsem,
                                     device_id=ydev, device_id_type=MESH).wait_recv()

    loads = []
    for j in range(6):
        rows = pl.ds(128 * j, 128)
        cp = pltpu.make_async_copy(inp.at[0, rows, :], own.at[rows, :], load_s.at[0, j])
        cp.start()
        loads.append(cp)

    @pl.when(is_nat)
    def _():
        for j in range(6):
            rows = pl.ds(128 * j, 128)
            pltpu.make_async_copy(cot.at[0, rows, :], toks.at[1, rows, :], load_s.at[1, j]).start()

    wown[...] = params[...].astype(BF16)
    moms[rep] = moment[...]

    barrier = pltpu.get_barrier_semaphore()
    group = [(2 * hi + (c + dc) % 2, fid(z, y, x + dx)) for dx in range(4) for dc in range(2) if dx or dc]
    group += [zdev[0], zdev[1], ydev, peers[1], peers[2]]
    for dev in group:
        pl.semaphore_signal(barrier, inc=1, device_id=dev, device_id_type=MESH)
    pl.semaphore_wait(barrier, len(group))

    for d in range(2):
        xd = c + 2 * d
        same = jnp.logical_and(xd == x, xh == c)
        dev = (2 * hi + xh, fid(z, y, xd))
        here = wts.at[:, z, y, kx, :, :]

        @pl.when(jnp.logical_not(same))
        def _(dev=dev, here=here, d=d):
            pltpu.make_async_remote_copy(src_ref=wown, dst_ref=here, send_sem=wx_s.at[d], recv_sem=wx_r.at[kx],
                                         device_id=dev, device_id_type=MESH).start()

        @pl.when(same)
        def _(here=here, d=d):
            pltpu.make_async_copy(wown, here, wx_s.at[d]).start()

    d0 = (nat * sib[0] + (1 - nat) * rep, fid(z, y, x + (1 - nat)))
    d1 = (sib[0], fid(z, y, x + 3 * (1 - nat)))

    def token_send(a, j):
        far = 768 + 256 * j if j < 3 else 768 + 256 * (j - 3) + 128
        rows = pl.ds(pl.multiple_of(nat * 128 * j + (1 - nat) * far, 128), 128)
        slot = j if j < 3 else j + 3 * (1 - nat)
        mine = pl.ds(128 * j, 128)
        src = own.at[mine, :] if a == 0 else cot.at[0, mine, :]
        send(src, toks.at[a, rows, :], tok_s.at[a, j], tok_r.at[a, slot], d0 if j < 3 else d1)

    def normalize(j):
        loads[j].wait()

        def body(i, carry):
            rows = pl.ds(pl.multiple_of(128 * j + 32 * i, 32), 32)
            wide = own[rows, :].astype(F32)
            out = (wide * lax.rsqrt(jnp.mean(wide * wide, axis=-1, keepdims=True) + norm_epsilon)).astype(BF16)
            own[rows, :] = out

            @pl.when(is_nat)
            def _():
                toks[0, rows, :] = out
            return carry
        lax.fori_loop(0, 4, body, 0)

    def tokens_out(js):
        for j in js:
            token_send(1, j)
        for j in js:
            normalize(j)
            token_send(0, j)

    for t, dev in enumerate(peers):
        send(moms.at[rep], moms.at[rep], om_s.at[t], om_r.at[t], dev)

    tokens_out((0, 3))

    for xl in range(2):
        here = wts.at[:, z, y, xl, :, :]
        same = jnp.logical_and(jnp.logical_and(is_nat, xh == c), kx == xl)

        @pl.when(jnp.logical_not(same))
        def _(here=here, xl=xl):
            recv(here, wx_s.at[0], wx_r.at[xl])

        @pl.when(same)
        def _(here=here):
            pltpu.make_async_copy(wown, here, wx_s.at[xh]).wait()

    def ga_region(k, off):
        return wts.at[k, zat(off), :, :, :, ZS]

    def ga_send(d, k, s):
        r = ga_region(k, -(s - 1) if d == 0 else s - 1)
        send(r, r, az_s.at[d, k, s - 1], az_r.at[d, k, s - 1], zdev[d])

    def ga_recv(d, k, s):
        recv(ga_region(k, -s if d == 0 else s), az_s.at[d, k, s - 1], az_r.at[d, k, s - 1])

    def gb_region(off, s, d):
        if s == 4:
            return wts.at[d, zat(off), y, :, :, YS]
        return wts.at[:, zat(off), y, :, :, YS]

    def gb_send(d, s):
        r = gb_region(-(s - 1) if d == 0 else s - 1, s, d)
        send(r, r, bz_s.at[d, s - 1], bz_r.at[d, s - 1], zdev[d])

    def gb_recv(d, s):
        recv(gb_region(-s if d == 0 else s, s, d), bz_s.at[d, s - 1], bz_r.at[d, s - 1])

    def by_region(slot, yy):
        if slot >= 7:
            return wts.at[slot - 7, zat(4), yy, :, :, YS]
        off = -slot if slot < 4 else slot - 3
        return wts.at[:, zat(off), yy, :, :, YS]

    def gby_send(slot):
        r = by_region(slot, y)
        send(r, r, by_s.at[slot], by_r.at[slot], ydev)

    def gby_recv(slot):
        recv(by_region(slot, yo), by_s.at[slot], by_r.at[slot])

    r = wts.at[:, z, y, :, :, ZS]
    send(r, r, ay_s.at[0], ay_r.at[0], ydev)
    gb_send(0, 1)
    gb_send(1, 1)
    gby_send(0)
    recv(wts.at[:, z, yo, :, :, ZS], ay_s.at[0], ay_r.at[0])
    for k in range(2):
        ga_send(0, k, 1)
        ga_send(1, k, 1)
    tokens_out((1, 4))
    for s in range(1, 4):
        for d in range(2):
            gb_recv(d, s)
            gb_send(d, s + 1)
            gby_send(s + 3 * d)
        for k in range(2):
            for d in range(2):
                ga_recv(d, k, s)
                if s < 3 or d == k:
                    ga_send(d, k, s + 1)
        if s == 1:
            tokens_out((2, 5))
    for d in range(2):
        gb_recv(d, 4)
        gby_send(7 + d)
    for d in range(2):
        ga_recv(d, d, 4)

    got = nat * 0 + (1 - nat) * 128
    give = nat * 128 + (1 - nat) * 0

    def forward(j):
        for a in range(2):
            rows = pl.ds(pl.multiple_of(768 + 256 * j + got, 128), 128)
            r = toks.at[a, rows, :]
            recv(r, tok_s.at[a, 0], tok_r.at[a, nat * j + (1 - nat) * (6 + j)])
            send(r, r, fwd_s.at[a, j], fwd_r.at[a, j], sib)

    def forwarded(j):
        for a in range(2):
            rows = pl.ds(pl.multiple_of(768 + 256 * j + give, 128), 128)
            recv(toks.at[a, rows, :], fwd_s.at[a, j], fwd_r.at[a, j])

    def values(group):
        def body(i, carry):
            k, rg = i // 2, i % 2
            tk = pl.ds(256 * group, 256)
            lhs = wts[k, pl.ds(4 * rg, 4), :, :, :, :].reshape(256, DW)
            out = lax.dot_general(lhs, toks[k, tk, :], (((1,), (1,)), ((), ())), preferred_element_type=F32)
            scale = jnp.where(k == 0, 1.0 / math.sqrt(DW), 1.0 / math.sqrt(HV)).astype(F32)
            vals[k, pl.ds(4 * rg, 4), :, :, :, tk] = (out * scale).astype(BF16).reshape(4, 2, 2, 16, 256)
            return carry
        lax.fori_loop(0, 4, body, 0)

    forward(0)
    forward(1)
    for slot in range(9):
        gby_recv(slot)

    @pl.when(is_nat)
    def _():
        for j in range(6):
            rows = pl.ds(128 * j, 128)
            pltpu.make_async_copy(cot.at[0, rows, :], toks.at[1, rows, :], load_s.at[1, j]).wait()

    @pl.when(jnp.logical_not(is_nat))
    def _():
        for j in range(6):
            for a in range(2):
                recv(toks.at[a, pl.ds(128 * j, 128), :], tok_s.at[a, 0], tok_r.at[a, j])

    values(0)
    values(1)
    values(2)
    forwarded(0)
    values(3)
    forward(2)
    forwarded(1)
    values(4)
    forwarded(2)
    values(5)

    def grad_z(offs):
        def body(k, carry):
            lhs = jnp.concatenate([vals[1 - k, zat(o)].reshape(64, PAIR) for o in offs], axis=0)
            out = jnp.dot(lhs, toks[k, :, 0:CZ], preferred_element_type=F32)
            for i, o in enumerate(offs):
                grad[k, zat(o), :, :, :, 0:CZ] = out[64 * i:64 * i + 64].reshape(2, 2, 16, CZ)
            return carry
        lax.fori_loop(0, 2, body, 0)

    def grad_y(offs, yy):
        def body(k, carry):
            lhs = jnp.concatenate([vals[1 - k, zat(o), yy].reshape(32, PAIR) for o in offs], axis=0)
            out = jnp.dot(lhs, toks[k, :, CZ:DW], preferred_element_type=F32)
            for i, o in enumerate(offs):
                grad[k, zat(o), yy, :, :, CZ:DW] = out[32 * i:32 * i + 32].reshape(2, 16, CY)
            return carry
        lax.fori_loop(0, 2, body, 0)

    def rz_first(slot, d, k, s, off):
        sz[slot] = grad[k, zat(off), :, :, :, 0:CZ].astype(BF16)
        send(sz.at[slot], rz.at[d, k, s - 1], cz_s.at[d, k, s - 1], cz_r.at[d, k, s - 1], zdev[d])

    def rz_hop(d, k, s):
        got = rz.at[d, k, s - 1]
        recv(got, cz_s.at[d, k, s - 1], cz_r.at[d, k, s - 1])
        off = 4 - s if d == 0 else s - 4
        rz[d, k, s - 1] = (rz[d, k, s - 1].astype(F32) + grad[k, zat(off), :, :, :, 0:CZ]).astype(BF16)
        send(got, rz.at[d, k, s], cz_s.at[d, k, s], cz_r.at[d, k, s], zdev[d])

    def ry_send(i):
        sy[i] = grad[:, zat(ORDER[i]), yo, :, :, CZ:DW].astype(BF16)
        send(sy.at[i], ry.at[i], cy_s.at[i], cy_r.at[i], ydev)

    def ry_recv(i):
        recv(ry.at[i], cy_s.at[i], cy_r.at[i])

    def r2_first():
        ry_recv(0)
        ry[0] = (ry[0].astype(F32) + grad[:, zat(4), y, :, :, CZ:DW]).astype(BF16)
        for d in range(2):
            send(ry.at[0, d], r2.at[d, 0, d], dz_s.at[d, 0], dz_r.at[d, 0], zdev[d])

    def r2_hop(d, s):
        off = 4 - s if d == 0 else s - 4
        i = ORDER.index(off % Z)
        ry_recv(i)
        if s == 1:
            recv(r2.at[d, 0, d], dz_s.at[d, 0], dz_r.at[d, 0])
            r2[d, 0, 1 - d] = (ry[i, 1 - d].astype(F32) + grad[1 - d, zat(off), y, :, :, CZ:DW]).astype(BF16)
            r2[d, 0, d] = (r2[d, 0, d].astype(F32) + ry[i, d].astype(F32)
                           + grad[d, zat(off), y, :, :, CZ:DW]).astype(BF16)
        else:
            recv(r2.at[d, s - 1], dz_s.at[d, s - 1], dz_r.at[d, s - 1])
            for k in range(2):
                r2[d, s - 1, k] = (r2[d, s - 1, k].astype(F32) + ry[i, k].astype(F32)
                                   + grad[k, zat(off), y, :, :, CZ:DW]).astype(BF16)
        send(r2.at[d, s - 1], r2.at[d, s], dz_s.at[d, s], dz_r.at[d, s], zdev[d])

    def owner_send(part, cols):
        for xl in range(2):
            xo = 2 * c + xl
            same = jnp.logical_and(xo == x, kx == c)
            src = fx.at[xl, :, :, cols]
            dst = xs.at[xh, :, :, cols]
            dev = (2 * hi + kx, fid(z, y, xo))

            @pl.when(jnp.logical_not(same))
            def _(src=src, dst=dst, dev=dev, xl=xl):
                pltpu.make_async_remote_copy(src_ref=src, dst_ref=dst, send_sem=ex_s.at[part, xl],
                                             recv_sem=ex_r.at[part, xh], device_id=dev, device_id_type=MESH).start()

            @pl.when(same)
            def _(src=src, dst=dst, xl=xl):
                pltpu.make_async_copy(src, dst, ex_s.at[part, xl]).start()

    def owner_wait(part, cols):
        for d in range(2):
            region = xs.at[d, :, :, cols]
            same = jnp.logical_and(is_nat, jnp.logical_and(xh == c, xh == d))

            @pl.when(jnp.logical_not(same))
            def _(region=region, d=d):
                recv(region, ex_s.at[part, 0], ex_r.at[part, d])
        for xl in range(2):
            same = jnp.logical_and(2 * c + xl == x, kx == c)
            src = fx.at[xl, :, :, cols]
            dst = xs.at[xh, :, :, cols]

            @pl.when(jnp.logical_not(same))
            def _(src=src, xl=xl):
                pltpu.make_async_remote_copy(src_ref=src, dst_ref=src, send_sem=ex_s.at[part, xl],
                                             recv_sem=ex_r.at[part, 0], device_id=ydev,
                                             device_id_type=MESH).wait_send()

            @pl.when(same)
            def _(src=src, dst=dst, xl=xl):
                pltpu.make_async_copy(src, dst, ex_s.at[part, xl]).wait()

    grad_z((4, 3))
    rz_first(0, 0, 0, 1, 4)
    rz_first(1, 1, 1, 1, 4)
    rz_first(2, 0, 1, 2, 3)
    grad_z((5, 2))
    rz_first(3, 1, 0, 2, 5)
    grad_y((4, 3, 5, 2), yo)
    for i in range(4):
        ry_send(i)
    grad_z((6, 1))
    rz_hop(0, 0, 1)
    rz_hop(1, 1, 1)
    grad_y((6, 1, 7, 0), yo)
    for i in range(4, 8):
        ry_send(i)
    grad_y((4, 3, 5, 2), y)
    rz_hop(0, 1, 2)
    rz_hop(1, 0, 2)
    r2_first()
    grad_z((7, 0))
    rz_hop(0, 0, 2)
    rz_hop(1, 1, 2)
    grad_y((6, 1, 7, 0), y)
    r2_hop(0, 1)
    r2_hop(1, 1)
    rz_hop(0, 1, 3)
    rz_hop(1, 0, 3)
    rz_hop(0, 0, 3)
    rz_hop(1, 1, 3)
    r2_hop(0, 2)
    r2_hop(1, 2)
    for d in range(2):
        for k in range(2):
            recv(rz.at[d, k, 3], cz_s.at[d, k, 3], cz_r.at[d, k, 3])
    for k in range(2):
        fs[k] = (grad[k, z, yo, :, :, 0:CZ] + rz[0, k, 3, yo].astype(F32)) + rz[1, k, 3, yo].astype(F32)
    send(fs, fr, dy_s.at[0], dy_r.at[0], ydev)
    for k in range(2):
        mine = (grad[k, z, y, :, :, 0:CZ] + rz[0, k, 3, y].astype(F32)) + rz[1, k, 3, y].astype(F32)
        for xl in range(2):
            fx[xl, k, :, 0:CZ] = mine[xl]
    r2_hop(0, 3)
    r2_hop(1, 3)
    recv(fr, dy_s.at[0], dy_r.at[0])
    for k in range(2):
        for xl in range(2):
            fx[xl, k, :, 0:CZ] = fx[xl, k, :, 0:CZ] + fr[k, xl]
    owner_send(0, ZS)
    ry_recv(7)
    for d in range(2):
        recv(r2.at[d, 3], dz_s.at[d, 3], dz_r.at[d, 3])
    for k in range(2):
        mine = ((grad[k, z, y, :, :, CZ:DW] + ry[7, k].astype(F32))
                + (r2[0, 3, k].astype(F32) + r2[1, 3, k].astype(F32)))
        for xl in range(2):
            fx[xl, k, :, CZ:DW] = mine[xl]
    owner_send(1, YS)
    owner_wait(0, ZS)
    owner_wait(1, YS)

    scale = inner_rate / math.sqrt(TOKENS)
    inner_o[...] = params[...] - scale * (xs[0] + xs[1])
    index = frag[0]
    pick = [inner_o[:, :, FRAGW * i:FRAGW * (i + 1)] for i in range(NFRAG)]
    osend[...] = jnp.where(index == 0, pick[0], jnp.where(index == 1, pick[1], pick[2]))
    for t, dev in enumerate(peers):
        send(osend, orecv.at[t], of_s.at[t], of_r.at[t], dev)
    for t in range(3):
        prep = (sib[0], peers[1][0], peers[2][0])[t]
        recv(moms.at[prep], om_s.at[t], om_r.at[t])
    moms_o[...] = moms[...]
    for t in range(3):
        recv(orecv.at[t], of_s.at[t], of_r.at[t])
    base = anchor[...]
    delta_o[...] = (((base - osend[...]) + (base - orecv[0])) + ((base - orecv[1]) + (base - orecv[2]))) * 0.25

    for d in range(2):
        xd = c + 2 * d
        same = jnp.logical_and(xd == x, xh == c)

        @pl.when(jnp.logical_not(same))
        def _(d=d):
            pltpu.make_async_remote_copy(src_ref=wown, dst_ref=wown, send_sem=wx_s.at[d], recv_sem=wx_r.at[0],
                                         device_id=ydev, device_id_type=MESH).wait_send()
    for cp in pending:
        cp.wait_send()


def window(inp, cot, params, anchor, moment, frag):
    dma = pltpu.SemaphoreType.DMA
    vmem = pltpu.VMEM
    both = lambda *shape: [dma(shape), dma(shape)]
    scratch = [
        vmem((2, PAIR, DW), BF16),
        vmem((TOK, DW), BF16),
        vmem((2, Z, Y, 2, ROWS, DW), BF16),
        vmem((2, ROWS, DW), BF16),
        vmem((2, Z, Y, 2, ROWS, PAIR), BF16),
        vmem((2, Z, Y, 2, ROWS, DW), F32),
        vmem((2, 2, 4, Y, 2, ROWS, CZ), BF16),
        vmem((4, Y, 2, ROWS, CZ), BF16),
        vmem((8, 2, 2, ROWS, CY), BF16),
        vmem((8, 2, 2, ROWS, CY), BF16),
        vmem((2, 4, 2, 2, ROWS, CY), BF16),
        vmem((2, 2, ROWS, CZ), F32),
        vmem((2, 2, ROWS, CZ), F32),
        vmem((2, 2, ROWS, DW), F32),
        vmem((2, 2, ROWS, DW), F32),
        vmem((2, ROWS, FRAGW), F32),
        vmem((3, 2, ROWS, FRAGW), F32),
        vmem((4, 2, ROWS, 256), F32),
        dma((2, 6)),
        dma((2, 6)), dma((2, 9)),
        *both(2, 3),
        *both(2),
        *both(1),
        *both(2, 2, 4),
        *both(2, 4),
        *both(9),
        *both(2, 2, 4),
        *both(8),
        *both(2, 4),
        *both(1),
        *both(2, 2),
        *both(3),
        *both(3),
    ]
    whole = pl.BlockSpec(memory_space=pltpu.VMEM)
    return pl.pallas_call(
        kernel,
        out_shape=(
            jax.ShapeDtypeStruct((2, ROWS, DW), F32),
            jax.ShapeDtypeStruct((2, ROWS, FRAGW), F32),
            jax.ShapeDtypeStruct((4, 2, ROWS, 256), F32),
        ),
        in_specs=[pl.BlockSpec(memory_space=pl.ANY)] * 2 + [whole] * 3 + [pl.BlockSpec(memory_space=pltpu.SMEM)],
        out_specs=(whole, whole, whole),
        scratch_shapes=scratch,
        cost_estimate=pl.CostEstimate(flops=4 * 2 * TOK * DW * HV, bytes_accessed=10**7, transcendentals=TOK),
        compiler_params=pltpu.CompilerParams(
            collective_id=1, has_side_effects=True, vmem_limit_bytes=58 * 2**20
        ),
    )(inp, cot, params, anchor, moment, frag)


def per_device(inputs, cotangent, replica_params, anchor, momentum, fragment):
    index = fragment[0]
    offset = index * FRAGW
    params = jnp.transpose(replica_params[0], (1, 0, 2))
    anchor_frag = lax.dynamic_slice_in_dim(anchor, offset, FRAGW, 2)
    piece = lax.dynamic_index_in_dim(momentum, index, 0, keepdims=False)
    padded = jnp.pad(jnp.transpose(piece, (1, 0, 2)), ((0, 0), (0, 0), (0, 256 - FRAGW // 4)))
    inner, delta, moms = window(
        inputs, cotangent, params, jnp.transpose(anchor_frag, (1, 0, 2)), padded, fragment
    )
    quarter = FRAGW // 4
    old = jnp.concatenate([moms[r, :, :, :quarter] for r in range(4)], axis=-1)
    new_moment = jnp.transpose(outer_momentum * old + delta, (1, 0, 2))
    delta = jnp.transpose(delta, (1, 0, 2))
    new_frag = anchor_frag - outer_rate * (delta + outer_momentum * new_moment)
    mine = lax.dynamic_slice_in_dim(new_moment, lax.axis_index("rep") * quarter, quarter, 2)
    zero = jnp.zeros((), jnp.int32)
    momentum_new = lax.dynamic_update_index_in_dim(momentum, mine, index, 0)
    anchor_new = lax.dynamic_update_slice(anchor, new_frag, (zero, zero, offset))
    inner = jnp.transpose(inner, (1, 0, 2))
    replica_new = lax.dynamic_update_slice(inner, new_frag, (zero, zero, offset))
    return (replica_new[None], anchor_new, momentum_new)


def solution(mesh):
    return jax.shard_map(
        per_device,
        mesh=mesh,
        in_specs=(
            P("rep", "fsdp", None),
            P("rep", "fsdp", None),
            P("rep", "fsdp", None, None),
            P("fsdp", None, None),
            P(None, "fsdp", None, "rep"),
            P(),
        ),
        out_specs=(
            P("rep", "fsdp", None, None),
            P("fsdp", None, None),
            P(None, "fsdp", None, "rep"),
        ),
        check_vma=False,
    )
```

time: 788 us -> 135 us (0.17)
  waiting for transfers between devices: 696 us -> 0 us
  Pallas kernels: 0 us -> 124 us
  matrix products: 22 us -> 0 us
  local copies, waits for them, and re-layouts: 29.5 us -> 8.52 us
  between operations: 14.5 us -> 1.34 us
  other arithmetic: 13.6 us -> 1.63 us
  blocking collectives: 10.9 us -> 0 us
    reduce_scatter x1 -> x0, waiting for transfers between devices: 346 us -> none  [per_device(): lax.psum_scatter(term(jnp.int32(0), rows_dev * lax.axis_size('fsdp')), 'f...]
    all_gather x1 -> x0, waiting for transfers between devices: 278 us -> none  [per_device(): piece = lax.all_gather(weights16, 'fsdp', axis=0, tiled=True)]
    pallas_call x0 -> x1, Pallas kernels: none -> 124 us  [window(): pl.pallas_call(kernel, out_shape=(jax.ShapeDtypeStruct((2, ROWS, DW), F32...]
    unnamed x4 -> x0, waiting for transfers between devices: 71.3 us -> none
    dot_general x4 -> x0, matrix products: 22 us -> none  [the longest x1 7.28 us: per_device(): jnp.einsum('td,kd->tk', normed, piece[:, 0, :], preferred_element_type=jn...]
    all_gather x1 -> x0, blocking collectives: 10.9 us -> none  [outer_update(): new_frag = lax.all_gather(new_piece, 'rep', axis=2, tiled=True)]
    unnamed x14 -> x9, local copies, waits for them, and re-layouts: 15.3 us -> 6.85 us
  transfers between devices with their start and end apart: 3 -> 0, of which waited for: 3 -> 0; matrix products, arithmetic and copies ran while one was open for 1% -> 0% of each run, Pallas kernels for 0% -> 0%
where the time goes in v1:
time: 135 us
  Pallas kernels  124 us (92%)
  local copies, waits for them, and re-layouts  8.52 us (6%)
  other arithmetic  1.63 us (1%)
    pallas_call x1, Pallas kernels, window(): pl.pallas_call(kernel, out_shape=(jax.ShapeDtypeStruct((2, ROWS, DW), F32...  124 us
    unnamed x9, local copies, waits for them, and re-layouts  6.85 us

profile of v1, /device:TPU:1, one launch (start us, length us, event | category | flops | bytes accessed | tf_op | source)
XLA Modules:
  0.0 135.2 jit_solution(7628836371169006718)
XLA Ops:
  0.6 1.0 copy.32
  1.6 0.9 copy.33
  3.2 0.6 copy.24
  3.8 0.6 pad.4.moment
  4.4 1.7 %copy.23 = f32[1,16,2,2304]{3,1,2,0:T(8,128)} copy(f32[1,16,2,2304]{3,2,1,0:T(2,128)} %param.8) | data formatting | bytes 589824 | tf_op args[2]
  6.1 123.7 %shard_map.85 = (f32[2,16,2304]{2,1,0:T(8,128)}, f32[2,16,768]{2,1,0:T(8,128)}, f32[4,2,16,256]{3,2,1,0:T(8,128)}) custom-call(bf16[1,768,2304]{2,1,0:T(8,128)(2,1)} %inp.1, bf16[1,768,2304]{2,1,0:T(8,128)(2,1)} %cot.1, f32[2,16,2304]{2,1,0:T(8,128)} %bitcast.39, f32[2,16,768]{2,1,0:T(8,128)} %bitcast.41, f32[2,16,256]{2,1,0:T(8,128)} %pad.4.moment, s32[1]{0:T(128)} %copy.31.frag), custom_call_target="tpu_custom_call" | custom-call | flops 14495514624 | bytes 10000000 | tf_op jit(solution)/shard_map/pallas_call | solution.py:504
  129.8 0.8 slice_bitcast_fusion.3
  130.6 1.6 %bitcast_dynamic-update-slice_fusion = (f32[1,16,2,2304]{3,1,2,0:T(8,128)}, f32[16,2,768]{2,0,1:T(8,128)S(1)}, f32[2,16,768]{2,1,0:T(8,128)S(1)}) fusion(f32[1,16,2,2304]{3,1,2,0:T(8,128)} %bitcast.38, s32[]{:T(128)S(6)} %select_n.14, f32[2,16,768]{2,1,0:T(8,128)} %get-tuple-element.7, f32[16,2,768]{2,1,0:T(2,128)S(1)} %constant_dynamic-slice_fusion.1, ...), kind=kLoop, calls=%fused_computation.3 | loop fusion | flops 221184 | bytes 589828 | tf_op jit(solution)/shard_map/dynamic_update_slice | solution.py:541
  132.3 0.1 copy_dynamic-update-slice_fusion
  132.4 0.0 copy-start
  132.4 2.0 %copy.14 = f32[1,16,2,2304]{3,2,1,0:T(2,128)} copy(f32[1,16,2,2304]{3,1,2,0:T(8,128)} %get-tuple-element.12) | data formatting | bytes 589824
  134.4 0.1 dynamic-slice_bitcast_fusion
  134.5 0.0 copy-done
  134.5 0.0 copy-start.1
  134.5 0.6 copy-done.1
  (4 shorter events, 0.1 us)
Async XLA Ops:
  132.4 2.1 %copy-start = (f32[16,2,2304]{2,1,0:T(2,128)}, f32[16,2,2304]{2,1,0:T(2,128)S(1)}, u32[]{:S(2)}) copy-start(f32[16,2,2304]{2,1,0:T(2,128)S(1)} %copy_dynamic-update-slice_fusion) | copy-start | bytes 884740
  134.5 0.6 copy-start.1

commit v2 on v1

v2 whole, which is shorter than its diff:
```python
import functools
import math

import jax
import jax.numpy as jnp
from jax import lax
from jax.experimental import pallas as pl
from jax.experimental.pallas import tpu as pltpu
from jax.sharding import PartitionSpec as P

DW = 2304
HV = 1024
NFRAG = 3
FRAGW = DW // NFRAG
QUARTER = FRAGW // 4
TOKENS = 49152
ROWS = 16
TOK = 768
PAIR = 2 * TOK
CZ = 1024
CY = DW - CZ
A0, B0, C0 = 0, 512, 1408
Z, Y, X = 8, 2, 4

inner_rate = 0.5
outer_rate = 0.7
outer_momentum = 0.9
norm_epsilon = 1e-06

MESH = pl.DeviceIdType.MESH
F32 = jnp.float32
BF16 = jnp.bfloat16
ZS = pl.ds(0, CZ)
YS = pl.ds(CZ, CY)
ORDER = (4, 3, 5, 2, 6, 1, 7, 0)


def kernel(inp, cot, params, anchor, moment, frag, inner_o, frag_o, moms_o,
           toks, own, wts, wown, vals, grad, rz, sz, ry, sy, r2, fs, fr, gs, gr, sc, fc, fx, xs, osend, orecv, moms,
           load_s, tok_s, tok_r, fwd_s, fwd_r, wx_s, wx_r, ay_s, ay_r, az_s, az_r, bz_s, bz_r, by_s, by_r,
           cz_s, cz_r, cy_s, cy_r, dz_s, dz_r, dy_s, dy_r, ex_s, ex_r, om_s, om_r, of_s, of_r):
    rep = lax.axis_index("rep")
    f = lax.axis_index("fsdp")
    hi, c = rep // 2, rep % 2
    z, y, x = f // 8, (f // 4) % 2, f % 4
    kx, xh = x % 2, x // 2
    nat = 1 - (c + kx) % 2
    is_nat = nat == 1
    yo = 1 - y

    def fid(zz, yy, xx):
        return (zz % Z) * 8 + yy * 4 + xx % X

    def zat(offset):
        return (z + offset) % Z

    sib = (2 * hi + 1 - c, f)
    zdev = ((rep, fid(z + 1, y, x)), (rep, fid(z + 7, y, x)))
    ydev = (rep, fid(z, yo, x))
    peers = (sib, (2 * (1 - hi) + c, f), (2 * (1 - hi) + 1 - c, f))

    pending = []

    def send(src, dst, ssem, rsem, dev):
        cp = pltpu.make_async_remote_copy(src_ref=src, dst_ref=dst, send_sem=ssem, recv_sem=rsem,
                                          device_id=dev, device_id_type=MESH)
        cp.start()
        pending.append(cp)
        return cp

    def recv(region, ssem, rsem):
        pltpu.make_async_remote_copy(src_ref=region, dst_ref=region, send_sem=ssem, recv_sem=rsem,
                                     device_id=ydev, device_id_type=MESH).wait_recv()

    barrier = pltpu.get_barrier_semaphore()
    group = [(2 * hi + (c + dc) % 2, fid(z, y, x + dx)) for dx in range(4) for dc in range(2) if dx or dc]
    group += [zdev[0], zdev[1], ydev, peers[1], peers[2]]
    for dev in group:
        pl.semaphore_signal(barrier, inc=1, device_id=dev, device_id_type=MESH)

    loads = []
    for j in range(6):
        rows = pl.ds(128 * j, 128)
        cp = pltpu.make_async_copy(inp.at[0, rows, :], own.at[rows, :], load_s.at[0, j])
        cp.start()
        loads.append(cp)

    @pl.when(is_nat)
    def _():
        for j in range(6):
            rows = pl.ds(128 * j, 128)
            pltpu.make_async_copy(cot.at[0, rows, :], toks.at[1, rows, :], load_s.at[1, j]).start()

    index = frag[0]
    for k in range(2):
        wown[k] = params[0, :, k, :].astype(BF16)
        moms[rep, k] = moment[index, :, k, :]
    pl.semaphore_wait(barrier, len(group))

    for d in range(2):
        xd = c + 2 * d
        same = jnp.logical_and(xd == x, xh == c)
        dev = (2 * hi + xh, fid(z, y, xd))
        here = wts.at[:, z, y, kx, :, :]

        @pl.when(jnp.logical_not(same))
        def _(dev=dev, here=here, d=d):
            pltpu.make_async_remote_copy(src_ref=wown, dst_ref=here, send_sem=wx_s.at[d], recv_sem=wx_r.at[kx],
                                         device_id=dev, device_id_type=MESH).start()

        @pl.when(same)
        def _(here=here, d=d):
            pltpu.make_async_copy(wown, here, wx_s.at[d]).start()

    d0 = (nat * sib[0] + (1 - nat) * rep, fid(z, y, x + (1 - nat)))
    d1 = (sib[0], fid(z, y, x + 3 * (1 - nat)))

    def token_send(a, j):
        far = 768 + 256 * j if j < 3 else 768 + 256 * (j - 3) + 128
        rows = pl.ds(pl.multiple_of(nat * 128 * j + (1 - nat) * far, 128), 128)
        slot = j if j < 3 else j + 3 * (1 - nat)
        mine = pl.ds(128 * j, 128)
        src = own.at[mine, :] if a == 0 else cot.at[0, mine, :]
        send(src, toks.at[a, rows, :], tok_s.at[a, j], tok_r.at[a, slot], d0 if j < 3 else d1)

    def normalize(j):
        loads[j].wait()

        def body(i, carry):
            rows = pl.ds(pl.multiple_of(128 * j + 32 * i, 32), 32)
            wide = own[rows, :].astype(F32)
            out = (wide * lax.rsqrt(jnp.mean(wide * wide, axis=-1, keepdims=True) + norm_epsilon)).astype(BF16)
            own[rows, :] = out

            @pl.when(is_nat)
            def _():
                toks[0, rows, :] = out
            return carry
        lax.fori_loop(0, 4, body, 0)

    def tokens_out(js):
        for j in js:
            token_send(1, j)
            token_send(0, j)

    for j in (0, 3):
        token_send(1, j)
    for j in (0, 3):
        normalize(j)
        token_send(0, j)
    for t, dev in enumerate(peers):
        send(moms.at[rep], moms.at[rep], om_s.at[t], om_r.at[t], dev)

    for xl in range(2):
        here = wts.at[:, z, y, xl, :, :]
        same = jnp.logical_and(jnp.logical_and(is_nat, xh == c), kx == xl)

        @pl.when(jnp.logical_not(same))
        def _(here=here, xl=xl):
            recv(here, wx_s.at[0], wx_r.at[xl])

        @pl.when(same)
        def _(here=here):
            pltpu.make_async_copy(wown, here, wx_s.at[xh]).wait()

    def ga_region(k, off):
        return wts.at[k, zat(off), :, :, :, ZS]

    def ga_send(d, k, s):
        r = ga_region(k, -(s - 1) if d == 0 else s - 1)
        send(r, r, az_s.at[d, k, s - 1], az_r.at[d, k, s - 1], zdev[d])

    def ga_recv(d, k, s):
        recv(ga_region(k, -s if d == 0 else s), az_s.at[d, k, s - 1], az_r.at[d, k, s - 1])

    def gb_region(off, s, d):
        if s == 4:
            return wts.at[d, zat(off), y, :, :, YS]
        return wts.at[:, zat(off), y, :, :, YS]

    def gb_send(d, s):
        r = gb_region(-(s - 1) if d == 0 else s - 1, s, d)
        send(r, r, bz_s.at[d, s - 1], bz_r.at[d, s - 1], zdev[d])

    def gb_recv(d, s):
        recv(gb_region(-s if d == 0 else s, s, d), bz_s.at[d, s - 1], bz_r.at[d, s - 1])

    def by_region(slot, yy):
        if slot >= 7:
            return wts.at[slot - 7, zat(4), yy, :, :, YS]
        off = -slot if slot < 4 else slot - 3
        return wts.at[:, zat(off), yy, :, :, YS]

    def gby_send(slot):
        r = by_region(slot, y)
        send(r, r, by_s.at[slot], by_r.at[slot], ydev)

    def gby_recv(slot):
        recv(by_region(slot, yo), by_s.at[slot], by_r.at[slot])

    got = (1 - nat) * 128
    give = nat * 128

    def forward(j):
        for a in range(2):
            rows = pl.ds(pl.multiple_of(768 + 256 * j + got, 128), 128)
            r = toks.at[a, rows, :]
            recv(r, tok_s.at[a, 0], tok_r.at[a, nat * j + (1 - nat) * (6 + j)])
            send(r, r, fwd_s.at[a, j], fwd_r.at[a, j], sib)

    def forwarded(j):
        for a in range(2):
            rows = pl.ds(pl.multiple_of(768 + 256 * j + give, 128), 128)
            recv(toks.at[a, rows, :], fwd_s.at[a, j], fwd_r.at[a, j])

    def own_tokens():
        @pl.when(is_nat)
        def _():
            for j in range(6):
                rows = pl.ds(128 * j, 128)
                pltpu.make_async_copy(cot.at[0, rows, :], toks.at[1, rows, :], load_s.at[1, j]).wait()

        @pl.when(jnp.logical_not(is_nat))
        def _():
            for j in range(6):
                for a in range(2):
                    recv(toks.at[a, pl.ds(128 * j, 128), :], tok_s.at[a, 0], tok_r.at[a, j])

    def values(first, count, offs):
        n = len(offs)

        def body(i, carry):
            k, group = i % 2, first + i // 2
            tk = pl.ds(pl.multiple_of(256 * group, 256), 256)
            lhs = jnp.concatenate([wts[k, zat(o)].reshape(64, DW) for o in offs], axis=0)
            out = lax.dot_general(lhs, toks[k, tk, :], (((1,), (1,)), ((), ())), preferred_element_type=F32)
            scale = jnp.where(k == 0, 1.0 / math.sqrt(DW), 1.0 / math.sqrt(HV)).astype(F32)
            out = (out * scale).astype(BF16)
            for b, o in enumerate(offs):
                vals[k, zat(o), :, :, :, tk] = out[64 * b:64 * b + 64].reshape(2, 2, 16, 256)
            return carry
        lax.fori_loop(0, 2 * count, body, 0)

    near, mid, far = (0, 1, 7), (2, 6), (3, 5, 4)

    r = wts.at[:, z, y, :, :, ZS]
    send(r, r, ay_s.at[0], ay_r.at[0], ydev)
    gb_send(0, 1)
    gb_send(1, 1)
    gby_send(0)
    normalize(1)
    normalize(4)
    recv(wts.at[:, z, yo, :, :, ZS], ay_s.at[0], ay_r.at[0])
    for k in range(2):
        ga_send(0, k, 1)
        ga_send(1, k, 1)
    normalize(2)
    normalize(5)

    def gather_step(s, work=()):
        work = list(work)

        def spare():
            if work:
                work.pop(0)()

        for d in range(2):
            gb_recv(d, s)
            if s < 4:
                gb_send(d, s + 1)
                gby_send(s + 3 * d)
            else:
                gby_send(7 + d)
            spare()
        for k in range(2):
            for d in range(2):
                if s < 4 or d == k:
                    ga_recv(d, k, s)
                    if s < 3 or (s == 3 and d == k):
                        ga_send(d, k, s + 1)
                    spare()
        for todo in work:
            todo()

    def value_work(first, count, offs):
        return lambda: values(first, count, offs)

    tokens_out((1, 4))
    gather_step(1)
    forward(0)
    tokens_out((2, 5))
    gather_step(2)
    own_tokens()
    for slot in (0, 1, 4):
        gby_recv(slot)
    gather_step(3, [value_work(g, 1, near) for g in range(3)])
    forward(1)
    forwarded(0)
    for slot in (2, 5):
        gby_recv(slot)
    gather_step(4, [value_work(3, 1, near)] + [value_work(g, 1, mid) for g in range(4)])
    for slot in (3, 6, 7, 8):
        gby_recv(slot)
    values(0, 4, far)
    forward(2)
    forwarded(1)
    values(4, 1, near + mid)
    values(4, 1, far)
    forwarded(2)
    values(5, 1, far)

    def grad_a(offs):
        def body(k, carry):
            lhs = jnp.concatenate([vals[1 - k, zat(o)].reshape(64, PAIR) for o in offs], axis=0)
            out = jnp.dot(lhs, toks[k, :, A0:B0], preferred_element_type=F32)
            for i, o in enumerate(offs):
                grad[k, zat(o), :, :, :, A0:B0] = out[64 * i:64 * i + 64].reshape(2, 2, 16, B0 - A0)
            return carry
        lax.fori_loop(0, 2, body, 0)

    def grad_b(yy):
        def body(k, carry):
            out = jnp.dot(vals[1 - k, :, yy].reshape(256, PAIR), toks[k, :, B0:C0], preferred_element_type=F32)
            grad[k, :, yy, :, :, B0:C0] = out.reshape(8, 2, 16, C0 - B0)
            return carry
        lax.fori_loop(0, 2, body, 0)

    def grad_c(xx):
        def body(k, carry):
            out = jnp.dot(vals[1 - k, :, :, xx].reshape(256, PAIR), toks[k, :, C0:DW], preferred_element_type=F32)
            grad[k, :, :, xx, :, C0:DW] = out.reshape(8, 2, 16, DW - C0)
            return carry
        lax.fori_loop(0, 2, body, 0)

    def rz_first(slot, d, k, s, off):
        sz[slot] = grad[k, zat(off), :, :, :, A0:B0].astype(BF16)
        send(sz.at[slot], rz.at[d, k, s - 1], cz_s.at[d, k, s - 1], cz_r.at[d, k, s - 1], zdev[d])

    def rz_hop(d, k, s):
        got = rz.at[d, k, s - 1]
        recv(got, cz_s.at[d, k, s - 1], cz_r.at[d, k, s - 1])
        off = 4 - s if d == 0 else s - 4
        rz[d, k, s - 1] = (rz[d, k, s - 1].astype(F32) + grad[k, zat(off), :, :, :, A0:B0]).astype(BF16)
        send(got, rz.at[d, k, s], cz_s.at[d, k, s], cz_r.at[d, k, s], zdev[d])

    xdev = (rep, fid(z, y, x + 2))

    def block(part, k, zz, own):
        if part == 0:
            return grad[k, zz, y if own else yo, :, :, B0:C0]
        return grad[k, zz, :, xh if own else 1 - xh, :, C0:DW]

    def half_send(part, i):
        for k in range(2):
            sy[part, i, k] = block(part, k, zat(ORDER[i]), False).astype(BF16)
        send(sy.at[part, i], ry.at[part, i], cy_s.at[part, i], cy_r.at[part, i], xdev if part else ydev)

    def half_recv(part, i):
        recv(ry.at[part, i], cy_s.at[part, i], cy_r.at[part, i])

    def r2_first(part):
        half_recv(part, 0)
        for k in range(2):
            ry[part, 0, k] = (ry[part, 0, k].astype(F32) + block(part, k, zat(4), True)).astype(BF16)
        for d in range(2):
            send(ry.at[part, 0, d], r2.at[part, d, 0, d], dz_s.at[part, d, 0], dz_r.at[part, d, 0], zdev[d])

    def r2_hop(part, d, s):
        off = (4 - s if d == 0 else s - 4) % Z
        i = ORDER.index(off)
        half_recv(part, i)
        if s == 1:
            recv(r2.at[part, d, 0, d], dz_s.at[part, d, 0], dz_r.at[part, d, 0])
        else:
            recv(r2.at[part, d, s - 1], dz_s.at[part, d, s - 1], dz_r.at[part, d, s - 1])
        for k in range(2):
            total = ry[part, i, k].astype(F32) + block(part, k, zat(off), True)
            if s > 1 or k == d:
                total = total + r2[part, d, s - 1, k].astype(F32)
            r2[part, d, s - 1, k] = total.astype(BF16)
        send(r2.at[part, d, s - 1], r2.at[part, d, s], dz_s.at[part, d, s], dz_r.at[part, d, s], zdev[d])

    def r2_last(part, k):
        return ((block(part, k, z, True) + ry[part, 7, k].astype(F32))
                + (r2[part, 0, 3, k].astype(F32) + r2[part, 1, 3, k].astype(F32)))

    def r2_end(part):
        half_recv(part, 7)
        for d in range(2):
            recv(r2.at[part, d, 3], dz_s.at[part, d, 3], dz_r.at[part, d, 3])

    cols = (pl.ds(A0, B0 - A0), pl.ds(B0, C0 - B0), pl.ds(C0, DW - C0))

    def owner_copies(part):
        out = []
        if part == 2:
            xo = 2 * c + xh
            out.append((fc, xs.at[0, :, :, cols[2]], 0, 0, xo))
        else:
            for xl in range(2):
                out.append((fx.at[xl, :, :, cols[part]], xs.at[xh, :, :, cols[part]], xl, xh, 2 * c + xl))
        return [o + (jnp.logical_and(o[4] == x, kx == c),) for o in out]

    def owner_send(part):
        for src, dst, i, j, xo, same in owner_copies(part):
            @pl.when(jnp.logical_not(same))
            def _(src=src, dst=dst, i=i, j=j, xo=xo):
                pltpu.make_async_remote_copy(src_ref=src, dst_ref=dst, send_sem=ex_s.at[part, i],
                                             recv_sem=ex_r.at[part, j], device_id=(2 * hi + kx, fid(z, y, xo)),
                                             device_id_type=MESH).start()

            @pl.when(same)
            def _(src=src, dst=dst, i=i):
                pltpu.make_async_copy(src, dst, ex_s.at[part, i]).start()

    def owner_wait(part):
        for d in range(1 if part == 2 else 2):
            region = xs.at[d, :, :, cols[part]]
            same = jnp.logical_and(is_nat, xh == c)
            if part < 2:
                same = jnp.logical_and(same, xh == d)

            @pl.when(jnp.logical_not(same))
            def _(region=region, d=d):
                recv(region, ex_s.at[part, 0], ex_r.at[part, d])
        for src, dst, i, j, xo, same in owner_copies(part):
            @pl.when(jnp.logical_not(same))
            def _(src=src, i=i):
                pltpu.make_async_remote_copy(src_ref=src, dst_ref=src, send_sem=ex_s.at[part, i],
                                             recv_sem=ex_r.at[part, 0], device_id=ydev,
                                             device_id_type=MESH).wait_send()

            @pl.when(same)
            def _(src=src, dst=dst, i=i):
                pltpu.make_async_copy(src, dst, ex_s.at[part, i]).wait()

    grad_a((4, 3, 5))
    rz_first(0, 0, 0, 1, 4)
    rz_first(1, 1, 1, 1, 4)
    rz_first(2, 0, 1, 2, 3)
    rz_first(3, 1, 0, 2, 5)
    values(5, 1, near + mid)
    grad_b(yo)
    for i in range(8):
        half_send(0, i)
    grad_c(1 - xh)
    for i in range(8):
        half_send(1, i)
    grad_a((2, 6, 1, 7, 0))
    rz_hop(0, 0, 1)
    rz_hop(1, 1, 1)
    grad_b(y)
    r2_first(0)
    rz_hop(0, 1, 2)
    rz_hop(1, 0, 2)
    grad_c(xh)
    r2_first(1)
    rz_hop(0, 0, 2)
    rz_hop(1, 1, 2)
    for part in range(2):
        r2_hop(part, 0, 1)
        r2_hop(part, 1, 1)
    rz_hop(0, 1, 3)
    rz_hop(1, 0, 3)
    rz_hop(0, 0, 3)
    rz_hop(1, 1, 3)
    for part in range(2):
        r2_hop(part, 0, 2)
        r2_hop(part, 1, 2)
    for d in range(2):
        for k in range(2):
            recv(rz.at[d, k, 3], cz_s.at[d, k, 3], cz_r.at[d, k, 3])
    for k in range(2):
        fs[k] = (grad[k, z, yo, :, :, A0:B0] + rz[0, k, 3, yo].astype(F32)) + rz[1, k, 3, yo].astype(F32)
    send(fs, fr, dy_s.at[0], dy_r.at[0], ydev)
    for k in range(2):
        mine = (grad[k, z, y, :, :, A0:B0] + rz[0, k, 3, y].astype(F32)) + rz[1, k, 3, y].astype(F32)
        for xl in range(2):
            fx[xl, k, :, A0:B0] = mine[xl]
    for part in range(2):
        r2_hop(part, 0, 3)
        r2_hop(part, 1, 3)
    recv(fr, dy_s.at[0], dy_r.at[0])
    for k in range(2):
        for xl in range(2):
            fx[xl, k, :, A0:B0] = fx[xl, k, :, A0:B0] + fr[k, xl]
    owner_send(0)
    r2_end(1)
    for k in range(2):
        mine = r2_last(1, k)
        sc[...] = mine
        gs[k] = sc[yo]
        fc[k] = sc[y]
    send(gs, gr, dy_s.at[1], dy_r.at[1], ydev)
    r2_end(0)
    for k in range(2):
        mine = r2_last(0, k)
        for xl in range(2):
            fx[xl, k, :, B0:C0] = mine[xl]
    owner_send(1)
    recv(gr, dy_s.at[1], dy_r.at[1])
    for k in range(2):
        fc[k] = fc[k] + gr[k]
    owner_send(2)
    for part in range(3):
        owner_wait(part)

    scale = inner_rate / math.sqrt(TOKENS)
    for k in range(2):
        inner_o[k, :, A0:C0] = params[0, :, k, A0:C0] - scale * (xs[0, k, :, A0:C0] + xs[1, k, :, A0:C0])
        inner_o[k, :, C0:DW] = params[0, :, k, C0:DW] - scale * xs[0, k, :, C0:DW]

    def fragment_of(array):
        pick = [array[:, FRAGW * i:FRAGW * (i + 1)] for i in range(NFRAG)]
        return jnp.where(index == 0, pick[0], jnp.where(index == 1, pick[1], pick[2]))

    for k in range(2):
        osend[k] = fragment_of(inner_o[k])
    for t, dev in enumerate(peers):
        send(osend, orecv.at[t], of_s.at[t], of_r.at[t], dev)
    for t in range(3):
        recv(moms.at[peers[t][0]], om_s.at[t], om_r.at[t])
    moms_o[...] = moms[...]
    for t in range(3):
        recv(orecv.at[t], of_s.at[t], of_r.at[t])
    for k in range(2):
        base = fragment_of(anchor[:, k, :])
        frag_o[k] = (((base - osend[k]) + (base - orecv[0, k])) + ((base - orecv[1, k]) + (base - orecv[2, k]))) * 0.25

    for d in range(2):
        xd = c + 2 * d
        same = jnp.logical_and(xd == x, xh == c)

        @pl.when(jnp.logical_not(same))
        def _(d=d):
            pltpu.make_async_remote_copy(src_ref=wown, dst_ref=wown, send_sem=wx_s.at[d], recv_sem=wx_r.at[0],
                                         device_id=ydev, device_id_type=MESH).wait_send()
    for cp in pending:
        cp.wait_send()


def window(inp, cot, params, anchor, moment, frag):
    dma = pltpu.SemaphoreType.DMA
    vmem = pltpu.VMEM
    both = lambda *shape: [dma(shape), dma(shape)]
    scratch = [
        vmem((2, PAIR, DW), BF16),
        vmem((TOK, DW), BF16),
        vmem((2, Z, Y, 2, ROWS, DW), BF16),
        vmem((2, ROWS, DW), BF16),
        vmem((2, Z, Y, 2, ROWS, PAIR), BF16),
        vmem((2, Z, Y, 2, ROWS, DW), F32),
        vmem((2, 2, 4, Y, 2, ROWS, B0 - A0), BF16),
        vmem((4, Y, 2, ROWS, B0 - A0), BF16),
        vmem((2, 8, 2, 2, ROWS, C0 - B0), BF16),
        vmem((2, 8, 2, 2, ROWS, C0 - B0), BF16),
        vmem((2, 2, 4, 2, 2, ROWS, C0 - B0), BF16),
        vmem((2, 2, ROWS, B0 - A0), F32),
        vmem((2, 2, ROWS, B0 - A0), F32),
        vmem((2, ROWS, DW - C0), F32),
        vmem((2, ROWS, DW - C0), F32),
        vmem((2, ROWS, DW - C0), F32),
        vmem((2, ROWS, DW - C0), F32),
        vmem((2, 2, ROWS, DW), F32),
        vmem((2, 2, ROWS, DW), F32),
        vmem((2, ROWS, FRAGW), F32),
        vmem((3, 2, ROWS, FRAGW), F32),
        vmem((4, 2, ROWS, QUARTER), F32),
        dma((2, 6)),
        dma((2, 6)), dma((2, 9)),
        *both(2, 3),
        *both(2),
        *both(1),
        *both(2, 2, 4),
        *both(2, 4),
        *both(9),
        *both(2, 2, 4),
        *both(2, 8),
        *both(2, 2, 4),
        *both(2),
        *both(3, 2),
        *both(3),
        *both(3),
    ]
    whole = pl.BlockSpec(memory_space=pltpu.VMEM)
    return pl.pallas_call(
        kernel,
        out_shape=(
            jax.ShapeDtypeStruct((2, ROWS, DW), F32),
            jax.ShapeDtypeStruct((2, ROWS, FRAGW), F32),
            jax.ShapeDtypeStruct((4, 2, ROWS, QUARTER), F32),
        ),
        in_specs=[pl.BlockSpec(memory_space=pl.ANY)] * 2 + [whole] * 3 + [pl.BlockSpec(memory_space=pltpu.SMEM)],
        out_specs=(whole, whole, whole),
        scratch_shapes=scratch,
        cost_estimate=pl.CostEstimate(flops=4 * 2 * TOK * DW * HV, bytes_accessed=10**7, transcendentals=TOK),
        compiler_params=pltpu.CompilerParams(
            collective_id=1, has_side_effects=True, vmem_limit_bytes=58 * 2**20
        ),
    )(inp, cot, params, anchor, moment, frag)


def finish(frag, inner, delta, moms, anchor, moment, replica_o, anchor_o, moment_o):
    index = frag[0]
    rep = lax.axis_index("rep")
    anchor_o[...] = anchor[...]
    moment_o[...] = moment[...]
    for k in range(2):
        change = delta[k]
        base = anchor[:, k, :]
        pick = [base[:, FRAGW * i:FRAGW * (i + 1)] for i in range(NFRAG)]
        base = jnp.where(index == 0, pick[0], jnp.where(index == 1, pick[1], pick[2]))
        old = jnp.concatenate([moms[r, k] for r in range(4)], axis=-1)
        new_moment = outer_momentum * old + change
        new_frag = base - outer_rate * (change + outer_momentum * new_moment)
        replica_o[0, :, k, :] = inner[k]
        for i in range(NFRAG):
            @pl.when(index == i)
            def _(i=i):
                replica_o[0, :, k, FRAGW * i:FRAGW * (i + 1)] = new_frag
                anchor_o[:, k, FRAGW * i:FRAGW * (i + 1)] = new_frag
        part = [new_moment[:, QUARTER * i:QUARTER * (i + 1)] for i in range(4)]
        low = jnp.where(rep == 0, part[0], part[1])
        high = jnp.where(rep == 2, part[2], part[3])
        moment_o[index, :, k, :] = jnp.where(rep < 2, low, high)


def per_device(inputs, cotangent, replica_params, anchor, momentum, fragment):
    inner, delta, moms = window(inputs, cotangent, replica_params, anchor, momentum, fragment)
    whole = pl.BlockSpec(memory_space=pltpu.VMEM)
    return pl.pallas_call(
        finish,
        out_shape=(
            jax.ShapeDtypeStruct((1, ROWS, 2, DW), F32),
            jax.ShapeDtypeStruct((ROWS, 2, DW), F32),
            jax.ShapeDtypeStruct((NFRAG, ROWS, 2, QUARTER), F32),
        ),
        in_specs=[pl.BlockSpec(memory_space=pltpu.SMEM)] + [whole] * 5,
        out_specs=(whole, whole, whole),
    )(fragment, inner, delta, moms, anchor, momentum)


def solution(mesh):
    return jax.shard_map(
        per_device,
        mesh=mesh,
        in_specs=(
            P("rep", "fsdp", None),
            P("rep", "fsdp", None),
            P("rep", "fsdp", None, None),
            P("fsdp", None, None),
            P(None, "fsdp", None, "rep"),
            P(),
        ),
        out_specs=(
            P("rep", "fsdp", None, None),
            P("fsdp", None, None),
            P(None, "fsdp", None, "rep"),
        ),
        check_vma=False,
    )
```

time: 135 us -> 119 us (0.88); the launches traced: 135 us -> 117 us
  local copies, waits for them, and re-layouts: 8.52 us -> 0 us
  Pallas kernels: 124 us -> 116 us
  other arithmetic: 1.63 us -> 0 us
    pallas_call x1, Pallas kernels: 124 us -> 113 us  [window(): pl.pallas_call(kernel, out_shape=(jax.ShapeDtypeStruct((2, ROWS, DW), F32...]
    unnamed x9 -> x0, local copies, waits for them, and re-layouts: 6.85 us -> none
    pallas_call x0 -> x1, Pallas kernels: none -> 2.25 us  [per_device(): pl.pallas_call(finish, out_shape=(jax.ShapeDtypeStruct((1, ROWS, 2, DW),...]
    dynamic_update_slice x1 -> x0, other arithmetic: 1.63 us -> none  [per_device(): lax.dynamic_update_slice(inner, new_frag, (zero, zero, offset))]
where the time goes in v2:
time: 119 us; the launch traced here: 117 us
  Pallas kernels  116 us (97%)
  between operations  1.29 us (1%)
    pallas_call x1, Pallas kernels, window(): pl.pallas_call(kernel, out_shape=(jax.ShapeDtypeStruct((2, ROWS, DW), F32...  113 us

profile of v2, /device:TPU:1, one launch (start us, length us, event | category | flops | bytes accessed | tf_op | source)
XLA Modules:
  0.0 117.0 jit_solution(16266889504041511053)
XLA Ops:
  1.3 113.5 %shard_map.85 = (f32[2,16,2304]{2,1,0:T(8,128)}, f32[2,16,768]{2,1,0:T(8,128)}, f32[4,2,16,192]{3,2,1,0:T(8,128)}) custom-call(bf16[1,768,2304]{2,1,0:T(8,128)(2,1)} %inp.1, bf16[1,768,2304]{2,1,0:T(8,128)(2,1)} %cot.1, f32[1,16,2,2304]{3,2,1,0:T(2,128)} %params.1, f32[16,2,2304]{2,1,0:T(2,128)} %anchor.3, f32[3,16,2,192]{3,2,1,0:T(2,128)} %moment.3, ...), custom_call_target="tpu_custom_call" | custom-call | flops 14495514624 | bytes 10000000 | tf_op jit(solution)/shard_map/pallas_call | solution.py:586
  114.8 2.2 %shard_map.86 = (f32[1,16,2,2304]{3,2,1,0:T(2,128)}, f32[16,2,2304]{2,1,0:T(2,128)}, f32[3,16,2,192]{3,2,1,0:T(2,128)}) custom-call(s32[1]{0:T(128)S(6)} %copy.9.frag, f32[2,16,2304]{2,1,0:T(8,128)} %get-tuple-element.6.inner, f32[2,16,768]{2,1,0:T(8,128)} %get-tuple-element.7.delta, f32[4,2,16,192]{3,2,1,0:T(8,128)} %get-tuple-element.8.moms, ...), custom_call_target="tpu_custom_call" | custom-call | tf_op jit(solution)/shard_map/pallas_call | solution.py:631

commit v3 on v2

--- a/solution.py
+++ b/solution.py
@@ -17,7 +17,7 @@
 ROWS = 16
 TOK = 768
 PAIR = 2 * TOK
-CZ = 1024
+CZ = 896
 CY = DW - CZ
 A0, B0, C0 = 0, 512, 1408
 Z, Y, X = 8, 2, 4
@@ -35,9 +35,9 @@
 ORDER = (4, 3, 5, 2, 6, 1, 7, 0)
 
 
-def kernel(inp, cot, params, anchor, moment, frag, inner_o, frag_o, moms_o,
-           toks, own, wts, wown, vals, grad, rz, sz, ry, sy, r2, fs, fr, gs, gr, sc, fc, fx, xs, osend, orecv, moms,
-           load_s, tok_s, tok_r, fwd_s, fwd_r, wx_s, wx_r, ay_s, ay_r, az_s, az_r, bz_s, bz_r, by_s, by_r,
+def kernel(inp, cot, params_h, anchor_h, moment_h, frag, inner_o, frag_o, moms_o,
+           toks, own, wts, wown, vals, grad, rz, sz, ry, sy, r2, fs, fr, fc, fx, xs, osend, orecv, moms, params, anchor, moment,
+           small_s, load_s, tok_s, tok_r, fwd_s, fwd_r, wx_s, wx_r, ay_s, ay_r, az_s, az_r, bz_s, bz_r, by_s, by_r,
            cz_s, cz_r, cy_s, cy_r, dz_s, dz_r, dy_s, dy_r, ex_s, ex_r, om_s, om_r, of_s, of_r):
     rep = lax.axis_index("rep")
     f = lax.axis_index("fsdp")
@@ -72,9 +72,14 @@
         pltpu.make_async_remote_copy(src_ref=region, dst_ref=region, send_sem=ssem, recv_sem=rsem,
                                      device_id=ydev, device_id_type=MESH).wait_recv()
 
+    small = [pltpu.make_async_copy(a, b, small_s.at[i])
+             for i, (a, b) in enumerate(((params_h, params), (moment_h, moment), (anchor_h, anchor)))]
+    for cp in small:
+        cp.start()
     barrier = pltpu.get_barrier_semaphore()
     group = [(2 * hi + (c + dc) % 2, fid(z, y, x + dx)) for dx in range(4) for dc in range(2) if dx or dc]
     group += [zdev[0], zdev[1], ydev, peers[1], peers[2]]
+    group += [(2 * hi + kx, fid(z, yo, 2 * c + xh)), (2 * hi + xh, fid(z, yo, 2 * kx + c))]
     for dev in group:
         pl.semaphore_signal(barrier, inc=1, device_id=dev, device_id_type=MESH)
 
@@ -92,6 +97,8 @@
             pltpu.make_async_copy(cot.at[0, rows, :], toks.at[1, rows, :], load_s.at[1, j]).start()
 
     index = frag[0]
+    small[0].wait()
+    small[1].wait()
     for k in range(2):
         wown[k] = params[0, :, k, :].astype(BF16)
         moms[rep, k] = moment[index, :, k, :]
@@ -101,16 +108,18 @@
         xd = c + 2 * d
         same = jnp.logical_and(xd == x, xh == c)
         dev = (2 * hi + xh, fid(z, y, xd))
-        here = wts.at[:, z, y, kx, :, :]
 
         @pl.when(jnp.logical_not(same))
-        def _(dev=dev, here=here, d=d):
-            pltpu.make_async_remote_copy(src_ref=wown, dst_ref=here, send_sem=wx_s.at[d], recv_sem=wx_r.at[kx],
-                                         device_id=dev, device_id_type=MESH).start()
+        def _(dev=dev, d=d):
+            for i, cut in enumerate((YS, ZS)):
+                pltpu.make_async_remote_copy(src_ref=wown.at[:, :, cut], dst_ref=wts.at[:, z, y, kx, :, cut],
+                                             send_sem=wx_s.at[i, d], recv_sem=wx_r.at[i, kx],
+                                             device_id=dev, device_id_type=MESH).start()
 
         @pl.when(same)
-        def _(here=here, d=d):
-            pltpu.make_async_copy(wown, here, wx_s.at[d]).start()
+        def _(d=d):
+            for i, cut in enumerate((YS, ZS)):
+                pltpu.make_async_copy(wown.at[:, :, cut], wts.at[:, z, y, kx, :, cut], wx_s.at[i, d]).start()
 
     d0 = (nat * sib[0] + (1 - nat) * rep, fid(z, y, x + (1 - nat)))
     d1 = (sib[0], fid(z, y, x + 3 * (1 - nat)))
@@ -144,27 +153,34 @@
             token_send(0, j)
 
     for j in (0, 3):
-        token_send(1, j)
-    for j in (0, 3):
         normalize(j)
-        token_send(0, j)
+    for d in range(2):
+        @pl.when(jnp.logical_not(jnp.logical_and(c + 2 * d == x, xh == c)))
+        def _(d=d):
+            for i, cut in enumerate((YS, ZS)):
+                part = wown.at[:, :, cut]
+                pltpu.make_async_remote_copy(src_ref=part, dst_ref=part, send_sem=wx_s.at[i, d], recv_sem=wx_r.at[i, 0],
+                                             device_id=ydev, device_id_type=MESH).wait_send()
+    tokens_out((0, 3))
     for t, dev in enumerate(peers):
         send(moms.at[rep], moms.at[rep], om_s.at[t], om_r.at[t], dev)
 
-    for xl in range(2):
-        here = wts.at[:, z, y, xl, :, :]
-        same = jnp.logical_and(jnp.logical_and(is_nat, xh == c), kx == xl)
-
-        @pl.when(jnp.logical_not(same))
-        def _(here=here, xl=xl):
-            recv(here, wx_s.at[0], wx_r.at[xl])
-
-        @pl.when(same)
-        def _(here=here):
-            pltpu.make_async_copy(wown, here, wx_s.at[xh]).wait()
+    def shards(i):
+        cut = (YS, ZS)[i]
+        for xl in range(2):
+            here = wts.at[:, z, y, xl, :, cut]
+            same = jnp.logical_and(jnp.logical_and(is_nat, xh == c), kx == xl)
+
+            @pl.when(jnp.logical_not(same))
+            def _(here=here, xl=xl):
+                recv(here, wx_s.at[i, 0], wx_r.at[i, xl])
+
+            @pl.when(same)
+            def _(here=here):
+                pltpu.make_async_copy(wown.at[:, :, cut], here, wx_s.at[i, xh]).wait()
 
     def ga_region(k, off):
-        return wts.at[k, zat(off), :, :, :, ZS]
+        return wts.at[:, zat(off), yo if k else y, :, :, ZS]
 
     def ga_send(d, k, s):
         r = ga_region(k, -(s - 1) if d == 0 else s - 1)
@@ -241,19 +257,32 @@
             return carry
         lax.fori_loop(0, 2 * count, body, 0)
 
+    def values_whole(group):
+        def body(k, carry):
+            tk = pl.ds(256 * group, 256)
+            out = lax.dot_general(wts[k].reshape(512, DW), toks[k, tk, :], (((1,), (1,)), ((), ())),
+                                  preferred_element_type=F32)
+            scale = jnp.where(k == 0, 1.0 / math.sqrt(DW), 1.0 / math.sqrt(HV)).astype(F32)
+            vals[k, :, :, :, :, tk] = (out * scale).astype(BF16).reshape(8, 2, 2, 16, 256)
+            return carry
+        lax.fori_loop(0, 2, body, 0)
+
     near, mid, far = (0, 1, 7), (2, 6), (3, 5, 4)
 
+    shards(0)
+    gb_send(0, 1)
+    gb_send(1, 1)
+    shards(1)
     r = wts.at[:, z, y, :, :, ZS]
     send(r, r, ay_s.at[0], ay_r.at[0], ydev)
-    gb_send(0, 1)
-    gb_send(1, 1)
+    ga_send(0, 0, 1)
+    ga_send(1, 0, 1)
     gby_send(0)
     normalize(1)
     normalize(4)
     recv(wts.at[:, z, yo, :, :, ZS], ay_s.at[0], ay_r.at[0])
-    for k in range(2):
-        ga_send(0, k, 1)
-        ga_send(1, k, 1)
+    ga_send(0, 1, 1)
+    ga_send(1, 1, 1)
     normalize(2)
     normalize(5)
 
@@ -304,10 +333,9 @@
     values(0, 4, far)
     forward(2)
     forwarded(1)
-    values(4, 1, near + mid)
-    values(4, 1, far)
+    values_whole(4)
     forwarded(2)
-    values(5, 1, far)
+    values_whole(5)
 
     def grad_a(offs):
         def body(k, carry):
@@ -394,19 +422,19 @@
     def owner_copies(part):
         out = []
         if part == 2:
-            xo = 2 * c + xh
-            out.append((fc, xs.at[0, :, :, cols[2]], 0, 0, xo))
+            for yy in range(2):
+                out.append((fc.at[yy], xs.at[y, :, :, cols[2]], yy, y, yy, 2 * c + xh))
         else:
             for xl in range(2):
-                out.append((fx.at[xl, :, :, cols[part]], xs.at[xh, :, :, cols[part]], xl, xh, 2 * c + xl))
-        return [o + (jnp.logical_and(o[4] == x, kx == c),) for o in out]
+                out.append((fx.at[xl, :, :, cols[part]], xs.at[xh, :, :, cols[part]], xl, xh, y, 2 * c + xl))
+        return [o + (jnp.logical_and(jnp.logical_and(o[5] == x, o[4] == y), kx == c),) for o in out]
 
     def owner_send(part):
-        for src, dst, i, j, xo, same in owner_copies(part):
+        for src, dst, i, j, yt, xo, same in owner_copies(part):
             @pl.when(jnp.logical_not(same))
-            def _(src=src, dst=dst, i=i, j=j, xo=xo):
+            def _(src=src, dst=dst, i=i, j=j, yt=yt, xo=xo):
                 pltpu.make_async_remote_copy(src_ref=src, dst_ref=dst, send_sem=ex_s.at[part, i],
-                                             recv_sem=ex_r.at[part, j], device_id=(2 * hi + kx, fid(z, y, xo)),
+                                             recv_sem=ex_r.at[part, j], device_id=(2 * hi + kx, fid(z, yt, xo)),
                                              device_id_type=MESH).start()
 
             @pl.when(same)
@@ -414,16 +442,14 @@
                 pltpu.make_async_copy(src, dst, ex_s.at[part, i]).start()
 
     def owner_wait(part):
-        for d in range(1 if part == 2 else 2):
+        for d in range(2):
             region = xs.at[d, :, :, cols[part]]
-            same = jnp.logical_and(is_nat, xh == c)
-            if part < 2:
-                same = jnp.logical_and(same, xh == d)
+            same = jnp.logical_and(jnp.logical_and(is_nat, xh == c), (xh if part < 2 else y) == d)
 
             @pl.when(jnp.logical_not(same))
             def _(region=region, d=d):
                 recv(region, ex_s.at[part, 0], ex_r.at[part, d])
-        for src, dst, i, j, xo, same in owner_copies(part):
+        for src, dst, i, j, yt, xo, same in owner_copies(part):
             @pl.when(jnp.logical_not(same))
             def _(src=src, i=i):
                 pltpu.make_async_remote_copy(src_ref=src, dst_ref=src, send_sem=ex_s.at[part, i],
@@ -439,32 +465,31 @@
     rz_first(1, 1, 1, 1, 4)
     rz_first(2, 0, 1, 2, 3)
     rz_first(3, 1, 0, 2, 5)
-    values(5, 1, near + mid)
+    grad_c(1 - xh)
+    for i in range(8):
+        half_send(1, i)
     grad_b(yo)
     for i in range(8):
         half_send(0, i)
-    grad_c(1 - xh)
-    for i in range(8):
-        half_send(1, i)
-    grad_a((2, 6, 1, 7, 0))
     rz_hop(0, 0, 1)
     rz_hop(1, 1, 1)
-    grad_b(y)
-    r2_first(0)
+    grad_a((2, 6, 1, 7, 0))
     rz_hop(0, 1, 2)
     rz_hop(1, 0, 2)
     grad_c(xh)
     r2_first(1)
     rz_hop(0, 0, 2)
     rz_hop(1, 1, 2)
-    for part in range(2):
+    grad_b(y)
+    r2_first(0)
+    for part in (1, 0):
         r2_hop(part, 0, 1)
         r2_hop(part, 1, 1)
     rz_hop(0, 1, 3)
     rz_hop(1, 0, 3)
     rz_hop(0, 0, 3)
     rz_hop(1, 1, 3)
-    for part in range(2):
+    for part in (1, 0):
         r2_hop(part, 0, 2)
         r2_hop(part, 1, 2)
     for d in range(2):
@@ -477,7 +502,7 @@
         mine = (grad[k, z, y, :, :, A0:B0] + rz[0, k, 3, y].astype(F32)) + rz[1, k, 3, y].astype(F32)
         for xl in range(2):
             fx[xl, k, :, A0:B0] = mine[xl]
-    for part in range(2):
+    for part in (1, 0):
         r2_hop(part, 0, 3)
         r2_hop(part, 1, 3)
     recv(fr, dy_s.at[0], dy_r.at[0])
@@ -488,27 +513,21 @@
     r2_end(1)
     for k in range(2):
         mine = r2_last(1, k)
-        sc[...] = mine
-        gs[k] = sc[yo]
-        fc[k] = sc[y]
-    send(gs, gr, dy_s.at[1], dy_r.at[1], ydev)
+        for yy in range(2):
+            fc[yy, k] = mine[yy]
+    owner_send(2)
     r2_end(0)
     for k in range(2):
         mine = r2_last(0, k)
         for xl in range(2):
             fx[xl, k, :, B0:C0] = mine[xl]
     owner_send(1)
-    recv(gr, dy_s.at[1], dy_r.at[1])
-    for k in range(2):
-        fc[k] = fc[k] + gr[k]
-    owner_send(2)
     for part in range(3):
         owner_wait(part)
 
     scale = inner_rate / math.sqrt(TOKENS)
     for k in range(2):
-        inner_o[k, :, A0:C0] = params[0, :, k, A0:C0] - scale * (xs[0, k, :, A0:C0] + xs[1, k, :, A0:C0])
-        inner_o[k, :, C0:DW] = params[0, :, k, C0:DW] - scale * xs[0, k, :, C0:DW]
+        inner_o[k] = params[0, :, k, :] - scale * (xs[0, k] + xs[1, k])
 
     def fragment_of(array):
         pick = [array[:, FRAGW * i:FRAGW * (i + 1)] for i in range(NFRAG)]
@@ -523,18 +542,11 @@
     moms_o[...] = moms[...]
     for t in range(3):
         recv(orecv.at[t], of_s.at[t], of_r.at[t])
+    small[2].wait()
     for k in range(2):
         base = fragment_of(anchor[:, k, :])
         frag_o[k] = (((base - osend[k]) + (base - orecv[0, k])) + ((base - orecv[1, k]) + (base - orecv[2, k]))) * 0.25
 
-    for d in range(2):
-        xd = c + 2 * d
-        same = jnp.logical_and(xd == x, xh == c)
-
-        @pl.when(jnp.logical_not(same))
-        def _(d=d):
-            pltpu.make_async_remote_copy(src_ref=wown, dst_ref=wown, send_sem=wx_s.at[d], recv_sem=wx_r.at[0],
-                                         device_id=ydev, device_id_type=MESH).wait_send()
     for cp in pending:
         cp.wait_send()
 
@@ -557,19 +569,20 @@
         vmem((2, 2, 4, 2, 2, ROWS, C0 - B0), BF16),
         vmem((2, 2, ROWS, B0 - A0), F32),
         vmem((2, 2, ROWS, B0 - A0), F32),
-        vmem((2, ROWS, DW - C0), F32),
-        vmem((2, ROWS, DW - C0), F32),
-        vmem((2, ROWS, DW - C0), F32),
-        vmem((2, ROWS, DW - C0), F32),
+        vmem((2, 2, ROWS, DW - C0), F32),
         vmem((2, 2, ROWS, DW), F32),
         vmem((2, 2, ROWS, DW), F32),
         vmem((2, ROWS, FRAGW), F32),
         vmem((3, 2, ROWS, FRAGW), F32),
         vmem((4, 2, ROWS, QUARTER), F32),
+        vmem((1, ROWS, 2, DW), F32),
+        vmem((ROWS, 2, DW), F32),
+        vmem((NFRAG, ROWS, 2, QUARTER), F32),
+        dma((3,)),
         dma((2, 6)),
         dma((2, 6)), dma((2, 9)),
         *both(2, 3),
-        *both(2),
+        *both(2, 2),
         *both(1),
         *both(2, 2, 4),
         *both(2, 4),
@@ -577,7 +590,7 @@
         *both(2, 2, 4),
         *both(2, 8),
         *both(2, 2, 4),
-        *both(2),
+        *both(1),
         *both(3, 2),
         *both(3),
         *both(3),
@@ -590,7 +603,7 @@
             jax.ShapeDtypeStruct((2, ROWS, FRAGW), F32),
             jax.ShapeDtypeStruct((4, 2, ROWS, QUARTER), F32),
         ),
-        in_specs=[pl.BlockSpec(memory_space=pl.ANY)] * 2 + [whole] * 3 + [pl.BlockSpec(memory_space=pltpu.SMEM)],
+        in_specs=[pl.BlockSpec(memory_space=pl.ANY)] * 5 + [pl.BlockSpec(memory_space=pltpu.SMEM)],
         out_specs=(whole, whole, whole),
         scratch_shapes=scratch,
         cost_estimate=pl.CostEstimate(flops=4 * 2 * TOK * DW * HV, bytes_accessed=10**7, transcendentals=TOK),

time: 119 us -> 112 us (0.941); the launches traced: 117 us -> 111 us
  Pallas kernels: 116 us -> 110 us
    pallas_call x1, Pallas kernels: 113 us -> 108 us  [window(): pl.pallas_call(kernel, out_shape=(jax.ShapeDtypeStruct((2, ROWS, DW), F32...]
where the time goes in v3:
time: 112 us; the launch traced here: 111 us
  Pallas kernels  110 us (98%)
  between operations  1.29 us (1%)
    pallas_call x1, Pallas kernels, window(): pl.pallas_call(kernel, out_shape=(jax.ShapeDtypeStruct((2, ROWS, DW), F32...  108 us
    pallas_call x1, Pallas kernels, per_device(): pl.pallas_call(finish, out_shape=(jax.ShapeDtypeStruct((1, ROWS, 2, DW),...  2.24 us

profile of v3, /device:TPU:1, one launch (start us, length us, event | category | flops | bytes accessed | tf_op | source)
XLA Modules:
  0.0 111.4 jit_solution(14811456606636372871)
XLA Ops:
  1.3 107.8 %shard_map.85 = (f32[2,16,2304]{2,1,0:T(8,128)}, f32[2,16,768]{2,1,0:T(8,128)}, f32[4,2,16,192]{3,2,1,0:T(8,128)}) custom-call(bf16[1,768,2304]{2,1,0:T(8,128)(2,1)} %inp.1, bf16[1,768,2304]{2,1,0:T(8,128)(2,1)} %cot.1, f32[1,16,2,2304]{3,2,1,0:T(2,128)} %params_h.1, f32[16,2,2304]{2,1,0:T(2,128)} %anchor.1, f32[3,16,2,192]{3,2,1,0:T(2,128)} %moment.1, ...), custom_call_target="tpu_custom_call" | custom-call | flops 14495514624 | bytes 10000000 | tf_op jit(solution)/shard_map/pallas_call | solution.py:599
  109.1 2.2 %shard_map.86 = (f32[1,16,2,2304]{3,2,1,0:T(2,128)}, f32[16,2,2304]{2,1,0:T(2,128)}, f32[3,16,2,192]{3,2,1,0:T(2,128)}) custom-call(s32[1]{0:T(128)S(6)} %copy.9.frag, f32[2,16,2304]{2,1,0:T(8,128)} %get-tuple-element.6.inner, f32[2,16,768]{2,1,0:T(8,128)} %get-tuple-element.7.delta, f32[4,2,16,192]{3,2,1,0:T(8,128)} %get-tuple-element.8.moms, ...), custom_call_target="tpu_custom_call" | custom-call | tf_op jit(solution)/shard_map/pallas_call | solution.py:644

commit v4 on v3

--- a/solution.py
+++ b/solution.py
@@ -322,12 +322,12 @@
     own_tokens()
     for slot in (0, 1, 4):
         gby_recv(slot)
-    gather_step(3, [value_work(g, 1, near) for g in range(3)])
+    gather_step(3)
     forward(1)
     forwarded(0)
     for slot in (2, 5):
         gby_recv(slot)
-    gather_step(4, [value_work(3, 1, near)] + [value_work(g, 1, mid) for g in range(4)])
+    gather_step(4, [value_work(g, 1, near + mid) for g in range(4)])
     for slot in (3, 6, 7, 8):
         gby_recv(slot)
     values(0, 4, far)

time: 112 us -> 111 us (level)
  no operation moved by 1% of the time
where the time goes in v4:
time: 111 us
  Pallas kernels  110 us (99%)
  between operations  1.29 us (1%)
    pallas_call x1, Pallas kernels, window(): pl.pallas_call(kernel, out_shape=(jax.ShapeDtypeStruct((2, ROWS, DW), F32...  108 us
    pallas_call x1, Pallas kernels, per_device(): pl.pallas_call(finish, out_shape=(jax.ShapeDtypeStruct((1, ROWS, 2, DW),...  2.25 us

profile of v4, /device:TPU:1, one launch (start us, length us, event | category | flops | bytes accessed | tf_op | source)
XLA Modules:
  0.0 111.1 jit_solution(2600366894895319833)
XLA Ops:
  1.3 107.5 %shard_map.85 = (f32[2,16,2304]{2,1,0:T(8,128)}, f32[2,16,768]{2,1,0:T(8,128)}, f32[4,2,16,192]{3,2,1,0:T(8,128)}) custom-call(bf16[1,768,2304]{2,1,0:T(8,128)(2,1)} %inp.1, bf16[1,768,2304]{2,1,0:T(8,128)(2,1)} %cot.1, f32[1,16,2,2304]{3,2,1,0:T(2,128)} %params_h.1, f32[16,2,2304]{2,1,0:T(2,128)} %anchor.1, f32[3,16,2,192]{3,2,1,0:T(2,128)} %moment.1, ...), custom_call_target="tpu_custom_call" | custom-call | flops 14495514624 | bytes 10000000 | tf_op jit(solution)/shard_map/pallas_call | solution.py:599
  108.8 2.2 %shard_map.86 = (f32[1,16,2,2304]{3,2,1,0:T(2,128)}, f32[16,2,2304]{2,1,0:T(2,128)}, f32[3,16,2,192]{3,2,1,0:T(2,128)}) custom-call(s32[1]{0:T(128)S(6)} %copy.9.frag, f32[2,16,2304]{2,1,0:T(8,128)} %get-tuple-element.6.inner, f32[2,16,768]{2,1,0:T(8,128)} %get-tuple-element.7.delta, f32[4,2,16,192]{3,2,1,0:T(8,128)} %get-tuple-element.8.moms, ...), custom_call_target="tpu_custom_call" | custom-call | tf_op jit(solution)/shard_map/pallas_call | solution.py:644

commit v5 on v4

--- a/solution.py
+++ b/solution.py
@@ -330,8 +330,9 @@
     gather_step(4, [value_work(g, 1, near + mid) for g in range(4)])
     for slot in (3, 6, 7, 8):
         gby_recv(slot)
-    values(0, 4, far)
+    values(0, 2, far)
     forward(2)
+    values(2, 2, far)
     forwarded(1)
     values_whole(4)
     forwarded(2)

time: 111 us -> 112 us (level)
  no operation moved by 1% of the time
where the time goes in v5:
time: 112 us
  Pallas kernels  111 us (99%)
  between operations  1.29 us (1%)
    pallas_call x1, Pallas kernels, window(): pl.pallas_call(kernel, out_shape=(jax.ShapeDtypeStruct((2, ROWS, DW), F32...  108 us
    pallas_call x1, Pallas kernels, per_device(): pl.pallas_call(finish, out_shape=(jax.ShapeDtypeStruct((1, ROWS, 2, DW),...  2.24 us

profile of v5, /device:TPU:1, one launch (start us, length us, event | category | flops | bytes accessed | tf_op | source)
XLA Modules:
  0.0 111.8 jit_solution(10538456137356385193)
XLA Ops:
  1.3 108.3 %shard_map.85 = (f32[2,16,2304]{2,1,0:T(8,128)}, f32[2,16,768]{2,1,0:T(8,128)}, f32[4,2,16,192]{3,2,1,0:T(8,128)}) custom-call(bf16[1,768,2304]{2,1,0:T(8,128)(2,1)} %inp.1, bf16[1,768,2304]{2,1,0:T(8,128)(2,1)} %cot.1, f32[1,16,2,2304]{3,2,1,0:T(2,128)} %params_h.1, f32[16,2,2304]{2,1,0:T(2,128)} %anchor.1, f32[3,16,2,192]{3,2,1,0:T(2,128)} %moment.1, ...), custom_call_target="tpu_custom_call" | custom-call | flops 14495514624 | bytes 10000000 | tf_op jit(solution)/shard_map/pallas_call | solution.py:600
  109.5 2.2 %shard_map.86 = (f32[1,16,2,2304]{3,2,1,0:T(2,128)}, f32[16,2,2304]{2,1,0:T(2,128)}, f32[3,16,2,192]{3,2,1,0:T(2,128)}) custom-call(s32[1]{0:T(128)S(6)} %copy.9.frag, f32[2,16,2304]{2,1,0:T(8,128)} %get-tuple-element.6.inner, f32[2,16,768]{2,1,0:T(8,128)} %get-tuple-element.7.delta, f32[4,2,16,192]{3,2,1,0:T(8,128)} %get-tuple-element.8.moms, ...), custom_call_target="tpu_custom_call" | custom-call | tf_op jit(solution)/shard_map/pallas_call | solution.py:645
